TPU v7x, 32 devices: a whole 2x2x4 slice. The times are simulated.
32 devices in a mesh: prow: 4 (over x, core), pcol: 8 (over z, y).
Axes of the slice: x: 2, y: 2, z: 4, core: 2. Of those that a mesh axis runs over, the one named last changes fastest.
Arguments:
- factor: bfloat16 [8, 4, 4, 8, 256, 256], P(None, 'prow', None, 'pcol')
- right_side: bfloat16 [4, 8, 256, 256], P(None, 'pcol'), may hold values from -6 to 6
- node_blocks: int32 [15], replicated, may hold values from 1 to 8, as said below
- front_mask: int32 [15, 32], replicated, may hold values from 0 to 1, as said below
Outputs:
- solution: bfloat16 [4, 8, 256, 256], P(None, 'pcol')
Inputs may be any that keep to these rules, and one draw needn't show every extreme that they name: node_blocks[s] counts the blocks of node s of a complete binary elimination tree in heap order (the parent of s is (s - 1) // 2); the nodes of one depth together have 8 blocks. front_mask[s, i] is 1 only where block i belongs to a strict ancestor of node s.
All inputs are finite; a program needn't handle non-finite values.
Results may differ from a plain program's by a relative error of at most 0.024.
Values may be sent and summed in bfloat16 or wider, within the bound.
A program may use at most 128 MiB of HBM per device.

v0:
```python
import jax
import jax.numpy as jnp
from jax import lax
from jax.sharding import PartitionSpec as P

LEVELS = 4


def node_order():
    ordering = []
    for depth_now in range(LEVELS - 1, -1, -1):
        ordering.extend(range(2**depth_now - 1, 2 ** (depth_now + 1) - 1))
    return ordering


def node_table(node_blocks, total_blocks):
    node_count = node_blocks.shape[0]
    ordered = jnp.array(node_order(), dtype=jnp.int32)
    node_ids = jnp.arange(node_count, dtype=jnp.int32)
    pick_sizes = (ordered[:, None] == node_ids[None, :]).astype(jnp.int32)
    level_sizes = jnp.sum(pick_sizes * node_blocks[None, :], axis=1)
    block_ends = jnp.cumsum(level_sizes)
    block_ids = jnp.arange(total_blocks, dtype=jnp.int32)
    positions = jnp.sum((block_ids[:, None] >= block_ends[None, :]).astype(jnp.int32), axis=1)
    return jnp.sum(
        (positions[:, None] == node_ids[None, :]).astype(jnp.int32) * ordered[None, :], axis=1
    )


def lookup(values_table, indices):
    positions_all = jnp.arange(values_table.shape[0], dtype=jnp.int32)
    return jnp.sum(
        (indices[:, None] == positions_all[None, :]).astype(jnp.int32) * values_table[None, :],
        axis=1,
    )


def panel_products(tile_stack, live_bits, vector):
    products = jnp.einsum("nxy,yw->nxw", tile_stack, vector, preferred_element_type=jnp.float32)
    return products * live_bits.astype(jnp.float32)[:, None, None]


def local(factor, right_side, node_blocks, front_mask):
    rows_local = factor.shape[0]
    cols_local = factor.shape[2]
    block_size = factor.shape[4]
    prow_count = lax.axis_size("prow")
    pcol_count = lax.axis_size("pcol")
    prow_index = lax.axis_index("prow")
    pcol_index = lax.axis_index("pcol")
    total_blocks = rows_local * prow_count
    level_rows = pcol_count // prow_count
    piece_rows = block_size // pcol_count
    tile_grid = factor.reshape(rows_local, cols_local, block_size, block_size)
    columns_in = right_side.reshape(cols_local, block_size, right_side.shape[3])
    block_node = node_table(node_blocks, total_blocks)
    row_ids = jnp.arange(rows_local, dtype=jnp.int32) * prow_count + prow_index
    col_ids = jnp.arange(cols_local, dtype=jnp.int32) * pcol_count + pcol_index
    row_nodes = lookup(block_node, row_ids)
    col_nodes = lookup(block_node, col_ids)
    node_ids = jnp.arange(node_blocks.shape[0], dtype=jnp.int32)
    pick_node = (col_nodes[:, None] == node_ids[None, :]).astype(jnp.int32)
    front_rows = jnp.sum(pick_node[:, :, None] * front_mask[None, :, :], axis=1)
    block_all = jnp.arange(total_blocks, dtype=jnp.int32)
    pick_row = (row_ids[:, None] == block_all[None, :]).astype(jnp.int32)
    front_bits = jnp.sum(pick_row[:, None, :] * front_rows[None, :, :], axis=2)
    diag_bits = (
        (row_nodes[:, None] == col_nodes[None, :]) & (row_ids[:, None] >= col_ids[None, :])
    ).astype(jnp.int32)

    def row_pieces(level_terms):
        rhs_width = level_terms.shape[2]
        split_rows = level_terms.reshape(level_rows, pcol_count, piece_rows, rhs_width)
        return jnp.transpose(split_rows, (1, 0, 2, 3))

    rhs_width = columns_in.shape[2]
    partial_value = jnp.zeros((rows_local, block_size, rhs_width), jnp.float32)
    solved_list = []
    for section_now in range(LEVELS):
        first_row = section_now * level_rows
        after_row = first_row + level_rows
        if section_now == 0:
            rhs_column = columns_in[0]
        else:
            mine = lax.psum_scatter(
                row_pieces(partial_value[first_row:after_row]).astype(jnp.bfloat16),
                "pcol",
                scatter_dimension=0,
                tiled=True,
            ).astype(jnp.float32)
            stacked = lax.all_gather(
                mine.reshape(level_rows, 1, piece_rows, rhs_width).astype(jnp.bfloat16),
                "prow",
                axis=1,
                tiled=True,
            ).astype(jnp.float32)
            arrived = lax.all_to_all(
                stacked.reshape(pcol_count, 1, piece_rows, rhs_width).astype(jnp.bfloat16),
                "pcol",
                split_axis=0,
                concat_axis=1,
                tiled=True,
            ).astype(jnp.float32)
            update = arrived.reshape(block_size, rhs_width)
            rhs_column = (columns_in[section_now].astype(jnp.float32) - update).astype(jnp.bfloat16)
        diag_terms = panel_products(
            tile_grid[first_row:after_row, section_now],
            diag_bits[first_row:after_row, section_now],
            rhs_column,
        )
        mine_solved = lax.psum_scatter(
            row_pieces(diag_terms).astype(jnp.bfloat16), "pcol", scatter_dimension=0, tiled=True
        )
        stacked_solved = lax.all_gather(
            mine_solved.reshape(level_rows, 1, piece_rows, rhs_width), "prow", axis=1, tiled=True
        )
        arrived_solved = lax.all_to_all(
            stacked_solved.reshape(pcol_count, 1, piece_rows, rhs_width),
            "pcol",
            split_axis=0,
            concat_axis=1,
            tiled=True,
        )
        solved = arrived_solved.reshape(block_size, rhs_width)
        solved_list.append(solved)
        if section_now + 1 < LEVELS:
            update_terms = panel_products(
                tile_grid[after_row:, section_now], front_bits[after_row:, section_now], solved
            )
            partial_value = partial_value.at[after_row:].add(update_terms)
    solution = jnp.stack(solved_list)
    return solution.reshape(cols_local, 1, block_size, columns_in.shape[2])


def solution(mesh):
    in_specs = (P(None, "prow", None, "pcol", None, None), P(None, "pcol", None, None), P(), P())
    out_specs = P(None, "pcol", None, None)
    return jax.shard_map(local, mesh=mesh, in_specs=in_specs, out_specs=out_specs, check_vma=False)
```

profile of v0, /device:TPU:0, one launch (start us, length us, event | category | flops | bytes accessed | tf_op | source)
XLA Modules:
  0.0 647.8 jit_solution(11800329941933548051)
XLA Ops:
  6.5 0.9 select_reduce_fusion.1
  7.4 0.2 reduce-window.8
  7.6 0.1 convert_reduce_fusion
  7.7 0.7 select_reduce_fusion
  8.4 0.2 select_reduce_fusion.3
  8.6 0.2 select_reduce_fusion.2
  8.8 0.1 and_convert_fusion
  8.9 0.1 convert_bitcast_fusion.6
  9.0 2.5 copy.38
  11.5 1.9 copy-done
  13.4 0.9 fusion.5
  14.4 0.1 multiply_reduce_fusion
  14.5 0.6 dynamic-slice.23
  15.1 0.1 fusion.24
  15.2 72.6 %all-reduce.15.cloned.1.call-done = bf16[8,2,32,256]{3,2,0,1:T(8,128)(2,1)} async-done(((bf16[8,2,32,256]{3,2,0,1:T(8,128)(2,1)}), bf16[8,2,32,256]{3,2,0,1:T(8,128)(2,1)}) %all-reduce.15.cloned.1.call-update) | async-done | bytes 262160
  87.8 1.3 constant_dynamic-slice_fusion.6
  89.1 5.9 all-gather
  95.0 3.9 all-to-all-start
  98.9 0.0 all-reduce.17.cloned.1.call-start
  98.9 0.1 multiply_reduce_fusion.1
  99.1 0.1 convert_bitcast_fusion.5
  99.2 7.2 %all-to-all-done = bf16[8,1,32,256]{3,2,1,0:T(8,128)(2,1)S(1)} async-done(((bf16[8,1,32,256]{3,2,1,0:T(8,128)(2,1)}), bf16[8,1,32,256]{3,2,1,0:T(8,128)(2,1)S(1)}, u32[]{:S(2)}, u32[]{:S(2)}) %all-to-all-start) | async-done | bytes 131104 | tf_op jit(solution)/shard_map/all_to_all | solution.py:117
  106.4 1.5 multiply_bitcast_fusion
  107.9 0.7 slice.215
  108.7 0.0 all-reduce.19.cloned.1.call-start
  108.7 68.8 %all-reduce.17.cloned.1.call-done = bf16[8,2,32,256]{3,2,0,1:T(8,128)(2,1)} async-done(((bf16[8,2,32,256]{3,2,0,1:T(8,128)(2,1)}), bf16[8,2,32,256]{3,2,0,1:T(8,128)(2,1)}) %all-reduce.17.cloned.1.call-update) | async-done | bytes 262160
  177.5 1.3 constant_dynamic-slice_fusion.5
  178.8 5.4 all-gather.1
  184.2 11.2 %all_to_all.28 = bf16[8,1,32,256]{3,2,1,0:T(8,128)(2,1)S(1)} all-to-all(bf16[8,1,32,256]{3,2,1,0:T(8,128)(2,1)S(1)} %bitcast.203), channel_id=1, replica_groups=mesh['prow'=4,'pcol'=8] {'pcol'}, dimensions={0} | all-to-all | bytes 262144 | tf_op jit(solution)/shard_map/all_to_all | solution.py:97
  195.4 1.9 fusion.6
  197.3 68.8 %all-reduce.19.cloned.1.call-done = bf16[8,2,32,256]{3,2,0,1:T(8,128)(2,1)} async-done(((bf16[8,2,32,256]{3,2,0,1:T(8,128)(2,1)}), bf16[8,2,32,256]{3,2,0,1:T(8,128)(2,1)}) %all-reduce.19.cloned.1.call-update) | async-done | bytes 262160
  266.1 1.3 constant_dynamic-slice_fusion.4
  267.4 5.9 all-gather.2
  273.3 3.9 all-to-all-start.2
  277.2 0.0 all-reduce.21.cloned.1.call-start
  277.3 0.1 convert_bitcast_fusion.3
  277.3 7.4 %all-to-all-done.2 = bf16[8,1,32,256]{3,2,1,0:T(8,128)(2,1)S(1)} async-done(((bf16[8,1,32,256]{3,2,1,0:T(8,128)(2,1)}), bf16[8,1,32,256]{3,2,1,0:T(8,128)(2,1)S(1)}, u32[]{:S(2)}, u32[]{:S(2)}) %all-to-all-start.2) | async-done | bytes 131104 | tf_op jit(solution)/shard_map/all_to_all | solution.py:117
  284.7 1.3 fusion.1
  286.1 0.7 slice.214
  286.8 0.0 all-reduce.23.cloned.1.call-start
  286.9 68.7 %all-reduce.21.cloned.1.call-done = bf16[8,2,32,256]{3,2,0,1:T(8,128)(2,1)} async-done(((bf16[8,2,32,256]{3,2,0,1:T(8,128)(2,1)}), bf16[8,2,32,256]{3,2,0,1:T(8,128)(2,1)}) %all-reduce.21.cloned.1.call-update) | async-done | bytes 262160
  355.6 1.3 constant_dynamic-slice_fusion.3
  356.9 5.4 all-gather.3
  362.4 11.2 %all_to_all.29 = bf16[8,1,32,256]{3,2,1,0:T(8,128)(2,1)S(1)} all-to-all(bf16[8,1,32,256]{3,2,1,0:T(8,128)(2,1)S(1)} %bitcast.204), channel_id=1, replica_groups=mesh['prow'=4,'pcol'=8] {'pcol'}, dimensions={0} | all-to-all | bytes 262144 | tf_op jit(solution)/shard_map/all_to_all | solution.py:97
  373.5 1.9 fusion.7
  375.4 68.8 %all-reduce.23.cloned.1.call-done = bf16[8,2,32,256]{3,2,0,1:T(8,128)(2,1)} async-done(((bf16[8,2,32,256]{3,2,0,1:T(8,128)(2,1)}), bf16[8,2,32,256]{3,2,0,1:T(8,128)(2,1)}) %all-reduce.23.cloned.1.call-update) | async-done | bytes 262160
  444.2 1.3 constant_dynamic-slice_fusion.2
  445.6 5.9 all-gather.4
  451.5 3.9 all-to-all-start.4
  455.3 0.0 all-reduce.25.cloned.1.call-start
  455.4 0.1 convert_bitcast_fusion.1
  455.5 7.4 %all-to-all-done.4 = bf16[8,1,32,256]{3,2,1,0:T(8,128)(2,1)S(1)} async-done(((bf16[8,1,32,256]{3,2,1,0:T(8,128)(2,1)}), bf16[8,1,32,256]{3,2,1,0:T(8,128)(2,1)S(1)}, u32[]{:S(2)}, u32[]{:S(2)}) %all-to-all-start.4) | async-done | bytes 131104 | tf_op jit(solution)/shard_map/all_to_all | solution.py:117
  462.8 1.9 fusion.4
  464.7 0.0 all-reduce.27.cloned.1.call-start
  464.8 68.7 %all-reduce.25.cloned.1.call-done = bf16[8,2,32,256]{3,2,0,1:T(8,128)(2,1)} async-done(((bf16[8,2,32,256]{3,2,0,1:T(8,128)(2,1)}), bf16[8,2,32,256]{3,2,0,1:T(8,128)(2,1)}) %all-reduce.25.cloned.1.call-update) | async-done | bytes 262160
  533.5 1.3 constant_dynamic-slice_fusion.1
  534.9 5.4 all-gather.5
  540.3 11.2 %all_to_all.30 = bf16[8,1,32,256]{3,2,1,0:T(8,128)(2,1)S(1)} all-to-all(bf16[8,1,32,256]{3,2,1,0:T(8,128)(2,1)S(1)} %bitcast.205), channel_id=1, replica_groups=mesh['prow'=4,'pcol'=8] {'pcol'}, dimensions={0} | all-to-all | bytes 262144 | tf_op jit(solution)/shard_map/all_to_all | solution.py:97
  551.5 1.9 fusion.8
  553.4 68.8 %all-reduce.27.cloned.1.call-done = bf16[8,2,32,256]{3,2,0,1:T(8,128)(2,1)} async-done(((bf16[8,2,32,256]{3,2,0,1:T(8,128)(2,1)}), bf16[8,2,32,256]{3,2,0,1:T(8,128)(2,1)}) %all-reduce.27.cloned.1.call-update) | async-done | bytes 262160
  622.2 1.3 constant_dynamic-slice_fusion
  623.5 5.4 all-gather.6
  628.9 11.2 %all_to_all.31 = bf16[8,1,32,256]{3,2,1,0:T(8,128)(2,1)S(1)} all-to-all(bf16[8,1,32,256]{3,2,1,0:T(8,128)(2,1)S(1)} %bitcast.206), channel_id=1, replica_groups=mesh['prow'=4,'pcol'=8] {'pcol'}, dimensions={0} | all-to-all | bytes 262144 | tf_op jit(solution)/shard_map/all_to_all | solution.py:117
  640.1 0.9 maximum_bitcast_fusion
  (18 shorter events, 0.1 us)
Async XLA Ops:
  6.5 81.2 %all-reduce.15.cloned.1.call-start = ((), (), s32[]{:S(2)}) async-start(), calls=%async_computation.7 | async-start | bytes 524288
  9.0 4.5 copy-start.2
  9.0 5.4 copy-start.1
  9.0 5.5 copy-start.3
  11.5 1.9 copy-start
  95.0 11.4 %all-to-all-start = ((bf16[8,1,32,256]{3,2,1,0:T(8,128)(2,1)}), bf16[8,1,32,256]{3,2,1,0:T(8,128)(2,1)S(1)}, u32[]{:S(2)}, u32[]{:S(2)}) async-start(bf16[8,1,32,256]{3,2,1,0:T(8,128)(2,1)} %bitcast.10), calls=%async_computation | async-start | bytes 262144 | tf_op jit(solution)/shard_map/all_to_all | solution.py:117
  98.9 78.6 %all-reduce.17.cloned.1.call-start = ((), (), s32[]{:S(2)}) async-start(), calls=%async_computation.8 | async-start | bytes 524288
  108.7 157.4 %all-reduce.19.cloned.1.call-start = ((), (), s32[]{:S(2)}) async-start(), calls=%async_computation.9 | async-start | bytes 524288
  273.3 11.4 %all-to-all-start.2 = ((bf16[8,1,32,256]{3,2,1,0:T(8,128)(2,1)}), bf16[8,1,32,256]{3,2,1,0:T(8,128)(2,1)S(1)}, u32[]{:S(2)}, u32[]{:S(2)}) async-start(bf16[8,1,32,256]{3,2,1,0:T(8,128)(2,1)} %bitcast.30), calls=%async_computation.2 | async-start | bytes 262144 | tf_op jit(solution)/shard_map/all_to_all | solution.py:117
  277.2 78.4 %all-reduce.21.cloned.1.call-start = ((), (), s32[]{:S(2)}) async-start(), calls=%async_computation.10 | async-start | bytes 524288
  286.8 157.4 %all-reduce.23.cloned.1.call-start = ((), (), s32[]{:S(2)}) async-start(), calls=%async_computation.11 | async-start | bytes 524288
  451.5 11.4 %all-to-all-start.4 = ((bf16[8,1,32,256]{3,2,1,0:T(8,128)(2,1)}), bf16[8,1,32,256]{3,2,1,0:T(8,128)(2,1)S(1)}, u32[]{:S(2)}, u32[]{:S(2)}) async-start(bf16[8,1,32,256]{3,2,1,0:T(8,128)(2,1)} %bitcast.50), calls=%async_computation.4 | async-start | bytes 262144 | tf_op jit(solution)/shard_map/all_to_all | solution.py:117
  455.3 78.2 %all-reduce.25.cloned.1.call-start = ((), (), s32[]{:S(2)}) async-start(), calls=%async_computation.12 | async-start | bytes 524288
  464.7 157.4 %all-reduce.27.cloned.1.call-start = ((), (), s32[]{:S(2)}) async-start(), calls=%async_computation.13 | async-start | bytes 524288
Sparse Core Ops, SparseCore 0:
  14.5 73.2 all-reduce.14
  108.8 68.6 all-reduce.16
  197.4 68.6 all-reduce.18
  286.9 68.6 all-reduce.20
  375.6 68.6 all-reduce.22
  464.9 68.6 all-reduce.24
  553.5 68.6 all-reduce.26
where the time goes:
time: 649 us; the launch traced here: 648 us
  waiting for transfers between devices  507 us (78%)
  blocking collectives  84 us (13%)
  local copies, waits for them, and re-layouts  15.9 us (2%)
  between operations  13.6 us (2%)
  starting transfers between devices  11.9 us (2%)
  matrix products  11.3 us (2%)
    unnamed x14, waiting for transfers between devices  485 us
    all_to_all x3, blocking collectives, local(): lax.all_to_all(stacked.reshape(pcol_count, 1, piece_rows, rhs_width).asty...  33.5 us
    all_gather x4, blocking collectives, local(): lax.all_gather(mine_solved.reshape(level_rows, 1, piece_rows, rhs_width),...  23.1 us
    all_to_all x3, waiting for transfers between devices, local(): lax.all_to_all(stacked_solved.reshape(pcol_count, 1, piece_rows, rhs_widt...  22 us
    all_gather x3, blocking collectives, local(): lax.all_gather(mine.reshape(level_rows, 1, piece_rows, rhs_width).astype(...  16.2 us
    unnamed x17, local copies, waits for them, and re-layouts  14.4 us
  transfers between devices with their start and end apart: 10, of which 10 were waited for; matrix products, arithmetic and copies ran while one was open for 0% of the time, Pallas kernels for 0%

commit v1 on v0

v1 whole, which is shorter than its diff:
```python
import functools

import jax
import jax.numpy as jnp
from jax import lax
from jax.experimental import pallas as pl
from jax.experimental.pallas import tpu as pltpu
from jax.sharding import PartitionSpec as P

MESH = pl.DeviceIdType.MESH
LANES = 128


def kernel(
    n_prow, n_pcol, factor, right, nodes, front, out,
    tiles, acc, parts, inbox, vec, load_sem, send_parts, recv_parts, send_vec, recv_vec,
):
    levels = right.shape[0]
    per_level = n_pcol // n_prow
    strip = vec.shape[3]
    chunks = vec.shape[1]
    size = strip * n_prow
    pr = lax.axis_index("prow")
    pc = lax.axis_index("pcol")

    def device(row, col):
        return {"prow": row, "pcol": col}

    barrier = pltpu.get_barrier_semaphore()
    home = lax.rem(pc, n_prow)
    for k in range(n_pcol):
        if k == 0:
            @pl.when(home != pr)
            def _():
                pl.semaphore_signal(barrier, inc=1, device_id=device(home, pc), device_id_type=MESH)
        else:
            source = lax.rem(pc + k, n_pcol)
            pl.semaphore_signal(barrier, inc=1, device_id=device(home, source), device_id_type=MESH)
    for k in range(1, n_prow):
        pl.semaphore_signal(
            barrier, inc=1, device_id=device(lax.rem(pr + k, n_prow), pc), device_id_type=MESH
        )

    loads = {}
    for g in range(levels):
        for h in range(g, -1, -1):
            loads[g, h] = pltpu.make_async_copy(
                factor.at[pl.ds(per_level * g, per_level), 0, h, 0],
                tiles.at[h, pl.ds(per_level * g, per_level)],
                load_sem.at[g, h],
            )
    loads[0, 0].start()
    for key in loads:
        if key != (0, 0):
            loads[key].start()

    ends = []
    for g in range(levels):
        first = 2 ** (levels - 1 - g) - 1
        total, ends_now = jnp.int32(0), []
        for k in range(first + 1):
            total = total + nodes[first + k]
            ends_now.append(total)
        ends.append(ends_now)

    def node(g, place):
        found = jnp.int32(2 ** (levels - 1 - g) - 1)
        for end in ends[g][:-1]:
            found = found + jnp.where(place >= end, 1, 0)
        return found

    col_node = [node(g, pc) for g in range(levels)]

    def row_place(r):
        return r * n_prow + pr

    def diag_bit(g, r):
        place = row_place(r)
        return jnp.where((node(g, place) == col_node[g]) & (place >= pc), 1.0, 0.0).astype(jnp.float32)

    def front_bit(g, h, r):
        return front[col_node[h], g * n_pcol + row_place(r)].astype(jnp.float32)

    def lanes(ch):
        return pl.ds(ch * LANES, LANES)

    order = [lax.rem(pc // n_prow + 1 + k, per_level) for k in range(per_level)]

    def part_copies(p, ch, r):
        place = row_place(r)
        copies = []
        for k in range(n_prow):
            s = lax.rem(pr + k, n_prow)
            copies.append(pltpu.make_async_remote_copy(
                src_ref=parts.at[p % 2, ch, r, s],
                dst_ref=inbox.at[p, ch, pc],
                send_sem=send_parts.at[p % 2, ch, r, s],
                recv_sem=recv_parts.at[p, ch, pc],
                device_id=device(s, place),
                device_id_type=MESH,
            ))
        return copies

    def guarded(p, r, action):
        if p % 2 == 0:
            pl.when(row_place(r) >= pc)(action)
        else:
            action()

    def send(p, ch, r):
        def go():
            for k, copy in enumerate(part_copies(p, ch, r)):
                if k == 0:
                    @pl.when(row_place(r) == pc)
                    def _():
                        pltpu.make_async_copy(
                            parts.at[p % 2, ch, r, pr], inbox.at[p, ch, pc], recv_parts.at[p, ch, pc]
                        ).start()
                    pl.when(row_place(r) != pc)(copy.start)
                else:
                    copy.start()
        guarded(p, r, go)

    def finish_sends(p, ch):
        for r in order:
            def go(r=r):
                for k, copy in enumerate(part_copies(p, ch, r)):
                    if k == 0:
                        pl.when(row_place(r) != pc)(copy.wait_send)
                    else:
                        copy.wait_send()
            guarded(p, r, go)
        for copy in vec_copies(p, ch):
            copy.wait_send()

    def vec_copies(p, ch):
        copies = []
        for k in range(1, n_prow):
            s = lax.rem(pr + k, n_prow)
            copies.append(pltpu.make_async_remote_copy(
                src_ref=vec.at[p, ch, pr],
                dst_ref=vec.at[p, ch, pr],
                send_sem=send_vec.at[p % 2, ch, s],
                recv_sem=recv_vec.at[p, ch, pr],
                device_id=device(s, pc),
                device_id_type=MESH,
            ))
        return copies

    def reduce_and_share(p, ch):
        def add(source, total):
            slot = inbox.at[p, ch, source]
            pltpu.make_async_remote_copy(
                src_ref=slot, dst_ref=slot, send_sem=send_vec.at[0, 0, 0],
                recv_sem=recv_parts.at[p, ch, source], device_id=device(pr, pc), device_id_type=MESH,
            ).wait_recv()
            return total + inbox[p, ch, source].astype(jnp.float32)

        total = jnp.zeros((strip, LANES), jnp.float32)
        if p % 2 == 0:
            total = lax.fori_loop(0, pc + 1, add, total)
        else:
            total = lax.fori_loop(0, n_pcol, add, total)
            rows = pl.ds(pl.multiple_of(pr * strip, strip), strip)
            total = right[(p + 1) // 2, 0, rows, lanes(ch)].astype(jnp.float32) - total
        vec[p, ch, pr] = total.astype(jnp.bfloat16)
        for copy in vec_copies(p, ch):
            copy.start()

    def receive(p, ch):
        for k in range(1, n_prow):
            s = lax.rem(pr + k, n_prow)
            slot = vec.at[p, ch, s]
            pltpu.make_async_remote_copy(
                src_ref=slot, dst_ref=slot, send_sem=send_vec.at[0, 0, 0],
                recv_sem=recv_vec.at[p, ch, s], device_id=device(pr, pc), device_id_type=MESH,
            ).wait_recv()
        return vec[p, ch].reshape(size, LANES)

    def product(g, h, r, x):
        return jnp.dot(tiles[h, per_level * g + r], x, preferred_element_type=jnp.float32)

    def put(p, ch, r, value):
        parts[p % 2, ch, r] = value.astype(jnp.bfloat16).reshape(n_prow, strip, LANES)
        send(p, ch, r)

    phases = 2 * levels - 1
    loads[0, 0].wait()
    for p in range(phases + 1):
        g = (p + 1) // 2
        values = []
        for ch in range(chunks):
            x = right[0, 0, :, lanes(ch)] if p == 0 else receive(p - 1, ch)
            values.append(x)
            if p % 2 == 1:
                out[g - 1, 0, :, lanes(ch)] = x
            if p == phases:
                continue
            if ch == 0 and p > 0:
                for h in ([g] if p % 2 == 0 else range(g)):
                    if p % 2 == 0 or h == g - 1:
                        loads[g, h].wait()
            for k, r in enumerate(order):
                if p % 2 == 0:
                    value = product(g, g, r, x) * diag_bit(g, r)
                else:
                    value = product(g, g - 1, r, x) * front_bit(g, g - 1, r)
                    if g > 1:
                        value = value + acc[g, ch, r]
                if p == 0 and ch == 0 and k == 0:
                    pl.semaphore_wait(barrier, n_pcol + n_prow - 2 + jnp.where(home != pr, 1, 0))
                put(p, ch, r, value)
        if p > 0:
            for ch in range(chunks):
                finish_sends(p - 1, ch)
        if p == phases:
            break
        if p % 2 == 1:
            h = g - 1
            for later in range(g + 1, levels):
                loads[later, h].wait()
                for ch in range(chunks):
                    for r in range(per_level):
                        value = product(later, h, r, values[ch]) * front_bit(later, h, r)
                        acc[later, ch, r] = value if h == 0 else acc[later, ch, r] + value
        for ch in range(chunks):
            reduce_and_share(p, ch)


def local(n_prow, n_pcol, factor, right_side, node_blocks, front_mask):
    levels, _, size, width = right_side.shape
    per_level = n_pcol // n_prow
    strip = size // n_prow
    chunks = width // LANES
    phases = 2 * levels - 1
    vmem = pl.BlockSpec(memory_space=pltpu.VMEM)
    smem = pl.BlockSpec(memory_space=pltpu.SMEM)
    dma = pltpu.SemaphoreType.DMA
    return pl.pallas_call(
        functools.partial(kernel, n_prow, n_pcol),
        out_shape=jax.ShapeDtypeStruct(right_side.shape, jnp.bfloat16),
        in_specs=[pl.BlockSpec(memory_space=pl.ANY), vmem, smem, smem],
        out_specs=vmem,
        scratch_shapes=[
            pltpu.VMEM((levels, levels * per_level, size, size), jnp.bfloat16),
            pltpu.VMEM((levels, chunks, per_level, size, LANES), jnp.float32),
            pltpu.VMEM((2, chunks, per_level, n_prow, strip, LANES), jnp.bfloat16),
            pltpu.VMEM((phases, chunks, n_pcol, strip, LANES), jnp.bfloat16),
            pltpu.VMEM((phases, chunks, n_prow, strip, LANES), jnp.bfloat16),
            dma((levels, levels)),
            dma((2, chunks, per_level, n_prow)),
            dma((phases, chunks, n_pcol)),
            dma((2, chunks, n_prow)),
            dma((phases, chunks, n_prow)),
        ],
        compiler_params=pltpu.CompilerParams(
            collective_id=0, has_side_effects=True, vmem_limit_bytes=40 * 2**20
        ),
    )(factor, right_side, node_blocks, front_mask)


def solution(mesh):
    in_specs = (P(None, "prow", None, "pcol", None, None), P(None, "pcol", None, None), P(), P())
    out_specs = P(None, "pcol", None, None)
    return jax.shard_map(
        functools.partial(local, mesh.shape["prow"], mesh.shape["pcol"]),
        mesh=mesh, in_specs=in_specs, out_specs=out_specs, check_vma=False,
    )
```

time: 649 us -> 98.3 us (0.15)
  waiting for transfers between devices: 507 us -> 0 us
  Pallas kernels: 0 us -> 91.3 us
  blocking collectives: 84 us -> 0 us
  between operations: 13.6 us -> 0.01 us
  starting transfers between devices: 11.9 us -> 0 us
  matrix products: 11.3 us -> 0 us
  local copies, waits for them, and re-layouts: 15.9 us -> 5.38 us
    unnamed x14 -> x0, waiting for transfers between devices: 485 us -> none
    pallas_call x0 -> x1, Pallas kernels: none -> 91.3 us  [local(): pl.pallas_call(functools.partial(kernel, n_prow, n_pcol), out_shape=jax.S...]
    all_to_all x4 -> x0, blocking collectives: 44.7 us -> none  [the longest x3 33.5 us: local(): lax.all_to_all(stacked.reshape(pcol_count, 1, piece_rows, rhs_width).asty...]
    all_gather x7 -> x0, blocking collectives: 39.3 us -> none  [the longest x4 23.1 us: local(): lax.all_gather(mine_solved.reshape(level_rows, 1, piece_rows, rhs_width),...]
    all_to_all x3 -> x0, waiting for transfers between devices: 22 us -> none  [local(): lax.all_to_all(stacked_solved.reshape(pcol_count, 1, piece_rows, rhs_widt...]
    all_to_all x3 -> x0, starting transfers between devices: 11.7 us -> none  [local(): lax.all_to_all(stacked_solved.reshape(pcol_count, 1, piece_rows, rhs_widt...]
    dot_general x7 -> x0, matrix products: 11.3 us -> none  [panel_products(): jnp.einsum('nxy,yw->nxw', tile_stack, vector, preferred_element_type=jnp....]
    unnamed x17 -> x9, local copies, waits for them, and re-layouts: 14.4 us -> 5.38 us
  transfers between devices with their start and end apart: 10 -> 0, of which waited for: 10 -> 0; matrix products, arithmetic and copies ran while one was open for 0% -> 0% of each run, Pallas kernels for 0% -> 0%
where the time goes in v1:
time: 98.3 us; the launch traced here: 96.7 us
  Pallas kernels  91.3 us (93%)
  local copies, waits for them, and re-layouts  5.38 us (5%)
    pallas_call x1, Pallas kernels, local(): pl.pallas_call(functools.partial(kernel, n_prow, n_pcol), out_shape=jax.S...  91.3 us
    unnamed x9, local copies, waits for them, and re-layouts  5.38 us

profile of v1, /device:TPU:0, one launch (start us, length us, event | category | flops | bytes accessed | tf_op | source)
XLA Modules:
  0.0 96.7 jit_solution(9500706000407942361)
XLA Ops:
  0.0 0.0 copy-start
  0.0 2.2 %copy-done = bf16[8,1,4,1,256,256]{5,4,3,2,1,0:T(8,128)(2,1)S(1)} copy-done((bf16[8,1,4,1,256,256]{5,4,3,2,1,0:T(8,128)(2,1)S(1)}, bf16[8,1,4,1,256,256]{5,4,3,2,1,0:T(8,128)(2,1)}, u32[]{:S(2)}) %copy-start) | copy-done | bytes 4194328
  2.2 0.0 copy-start.1
  2.2 1.0 %copy-done.1 = bf16[4,1,256,256]{3,2,1,0:T(8,128)(2,1)S(1)} copy-done((bf16[4,1,256,256]{3,2,1,0:T(8,128)(2,1)S(1)}, bf16[4,1,256,256]{3,2,1,0:T(8,128)(2,1)}, u32[]{:S(2)}) %copy-start.1) | copy-done | bytes 524312
  3.2 0.0 copy-start.2
  3.2 0.7 copy-done.2
  3.9 0.0 copy-start.3
  3.9 0.7 copy-done.3
  4.6 91.3 %shard_map.46 = bf16[4,1,256,256]{3,2,1,0:T(8,128)(2,1)S(1)} custom-call(bf16[8,1,4,1,256,256]{5,4,3,2,1,0:T(8,128)(2,1)S(1)} %copy-done, bf16[4,1,256,256]{3,2,1,0:T(8,128)(2,1)S(1)} %copy-done.1, s32[15]{0:T(128)S(1)} %copy-done.3, s32[15,32]{1,0:T(8,128)S(1)} %copy-done.2), custom_call_target="tpu_custom_call" | custom-call | tf_op jit(solution)/shard_map/pallas_call | solution.py:239
  95.9 0.8 copy.6
Async XLA Ops:
  0.0 2.2 %copy-start = (bf16[8,1,4,1,256,256]{5,4,3,2,1,0:T(8,128)(2,1)S(1)}, bf16[8,1,4,1,256,256]{5,4,3,2,1,0:T(8,128)(2,1)}, u32[]{:S(2)}) copy-start(bf16[8,1,4,1,256,256]{5,4,3,2,1,0:T(8,128)(2,1)} %factor.1) | copy-start | bytes 12582916
  2.2 1.0 %copy-start.1 = (bf16[4,1,256,256]{3,2,1,0:T(8,128)(2,1)S(1)}, bf16[4,1,256,256]{3,2,1,0:T(8,128)(2,1)}, u32[]{:S(2)}) copy-start(bf16[4,1,256,256]{3,2,1,0:T(8,128)(2,1)} %right.1) | copy-start | bytes 1572868
  3.2 0.7 copy-start.2
  3.9 0.7 copy-start.3

commit v2 on v0

v2 whole, which is shorter than its diff:
```python
import functools

import jax
import jax.numpy as jnp
from jax import lax
from jax.experimental import pallas as pl
from jax.experimental.pallas import tpu as pltpu
from jax.sharding import PartitionSpec as P

MESH = pl.DeviceIdType.MESH
CHUNKS = 2


def pair(g, h):
    return g * (g + 1) // 2 + h


def dot_nt(a, b):
    return lax.dot_general(a, b, (((1,), (1,)), ((), ())), preferred_element_type=jnp.float32)


def kernel(
    n_prow, n_pcol, factor, right, nodes, front, out,
    tiles, flat, turned, acc, first, parts, inbox, solved,
    load_sem, flat_sem, tile_send, relay_send, tile_recv,
    first_send, part_send, part_recv, share_send, share_recv,
):
    levels, _, size, width = right.shape
    per_level = n_pcol // n_prow
    rows = width // n_prow // CHUNKS
    pairs = n_prow // 2 - 1
    phases = 2 * levels - 1
    pr = lax.axis_index("prow")
    pc = lax.axis_index("pcol")
    near = pr + 1 - 2 * lax.rem(pr, 2)

    def device(row, col):
        return {"prow": row, "pcol": col}

    def remote(src, dst, send, recv, row, col):
        return pltpu.make_async_remote_copy(
            src_ref=src, dst_ref=dst, send_sem=send, recv_sem=recv,
            device_id=device(row, col), device_id_type=MESH,
        )

    def arrived(slot, sem):
        remote(slot, slot, share_send.at[0, 0, 0], sem, pr, pc).wait_recv()

    barrier = pltpu.get_barrier_semaphore()
    home = lax.rem(pc, n_prow)

    def greet(row, col):
        pl.semaphore_signal(barrier, inc=1, device_id=device(row, col), device_id_type=MESH)

    for k in range(1, n_prow):
        greet(lax.rem(pr + k, n_prow), pc)
    for k in range(1, n_pcol):
        greet(pr, lax.rem(pc + k, n_pcol))

    @pl.when(home != pr)
    def _():
        for k in range(n_pcol):
            greet(home, lax.rem(pc + k, n_pcol))

    def place(r):
        return r * n_prow + pr

    def load(g, h, r):
        return pltpu.make_async_copy(
            factor.at[per_level * g + r, 0, h, 0], tiles.at[pair(g, h), place(r)],
            load_sem.at[pair(g, h), r],
        )

    flat_copy = pltpu.make_async_copy(right.at[:, 0], flat, flat_sem)
    flat_copy.start()
    for g in range(levels):
        for h in range(g + 1):
            for r in range(per_level):
                load(g, h, r).start()

    ends = []
    for g in range(levels):
        base = 2 ** (levels - 1 - g) - 1
        total, ends_now = jnp.int32(0), []
        for k in range(base + 1):
            total = total + nodes[base + k]
            ends_now.append(total)
        ends.append(ends_now)

    def node(g, i):
        found = jnp.int32(2 ** (levels - 1 - g) - 1)
        for end in ends[g][:-1]:
            found = found + jnp.where(i >= end, 1, 0)
        return found

    col_node = [node(g, pc) for g in range(levels)]

    def diag_bit(g, i):
        return jnp.where((node(g, i) == col_node[g]) & (i >= pc), 1.0, 0.0).astype(jnp.float32)

    def front_bit(g, h, i):
        return front[col_node[h], g * n_pcol + i].astype(jnp.float32)

    def live(g, h, i, action):
        if g == h:
            pl.when(i >= pc)(action)
        else:
            action()

    def tile_copies(g, h, r):
        q, i = pair(g, h), place(r)
        targets = [lax.rem(pr + 2 * k, n_prow) for k in range(1, pairs + 1)] + [near]
        return [
            remote(factor.at[per_level * g + r, 0, h, 0], tiles.at[q, i],
                   tile_send.at[q, r, k], tile_recv.at[q, i], target, pc)
            for k, target in enumerate(targets)
        ]

    def relay_copies(g, h, r):
        q = pair(g, h)
        copies = []
        for k in range(1, pairs + 1):
            i = r * n_prow + lax.rem(pr + 2 * k, n_prow)
            copies.append((i, remote(tiles.at[q, i], tiles.at[q, i], relay_send.at[q, r, k - 1],
                                     tile_recv.at[q, i], near, pc)))
        return copies

    def issue(g, h):
        for r in range(per_level):
            def go(r=r):
                for copy in tile_copies(g, h, r):
                    copy.start()
            live(g, h, place(r), go)

    def relay(g, h):
        for r in range(per_level):
            for i, copy in relay_copies(g, h, r):
                def go(i=i, copy=copy):
                    arrived(tiles.at[pair(g, h), i], tile_recv.at[pair(g, h), i])
                    copy.start()
                live(g, h, i, go)

    def collect(g, h):
        q = pair(g, h)
        for r in range(per_level):
            load(g, h, r).wait()
            for k in range(pairs + 1):
                i = r * n_prow + lax.rem(near + 2 * k, n_prow)
                live(g, h, i, lambda i=i: arrived(tiles.at[q, i], tile_recv.at[q, i]))

    def settle(g, h):
        for r in range(per_level):
            def go(r=r):
                for copy in tile_copies(g, h, r):
                    copy.wait_send()
            live(g, h, place(r), go)
            for i, copy in relay_copies(g, h, r):
                live(g, h, i, copy.wait_send)

    def first_copies(r, ch):
        return [
            remote(first.at[r, s, ch], inbox.at[0, ch, pc], first_send.at[r, s, ch],
                   part_recv.at[0, ch, pc], s, place(r))
            for s in [lax.rem(pr + k, n_prow) for k in range(n_prow)]
        ]

    def first_each(r, ch, action, stay):
        for k, copy in enumerate(first_copies(r, ch)):
            if k == 0:
                pl.when(place(r) != pc)(lambda: action(copy))
                if stay is not None:
                    pl.when(place(r) == pc)(stay)
            else:
                action(copy)

    far = [lax.rem(pc // n_prow + 1 + k, per_level) for k in range(per_level)]

    def first_phase():
        for r in far:
            i = place(r)

            @pl.when(i >= pc)
            def _():
                value = dot_nt(turned[0], tiles[0, i]) * diag_bit(0, i)
                first[r] = value.astype(jnp.bfloat16).reshape(n_prow, CHUNKS, rows, size)
                for ch in range(CHUNKS):
                    def stay(ch=ch):
                        inbox[0, ch, pc] = first[r, pr, ch]
                    first_each(r, ch, lambda copy: copy.start(), stay)

    def first_settle():
        for r in far:
            @pl.when(place(r) >= pc)
            def _():
                for ch in range(CHUNKS):
                    first_each(r, ch, lambda copy: copy.wait_send(), None)

    def part_copy(p, ch, i):
        return remote(parts.at[p % 2, ch, i], inbox.at[p, ch, pc], part_send.at[p % 2, ch, i],
                      part_recv.at[p, ch, pc], pr, i)

    def each_row(body):
        def step(k):
            return lax.rem(pc + n_pcol // 2 + k, n_pcol)

        if n_pcol <= 8:
            for k in range(n_pcol):
                if k != n_pcol // 2:
                    body(step(k))
        else:
            def loop(k, carry):
                i = step(k)
                pl.when(i != pc)(lambda: body(i))
                return carry

            lax.fori_loop(0, n_pcol, loop, 0)

    def products(p, ch, x):
        g = (p + 1) // 2
        h = g if p % 2 == 0 else g - 1

        def result(i):
            value = dot_nt(x, tiles[pair(g, h), i])
            if p % 2 == 0:
                return value * diag_bit(g, i)
            value = value * front_bit(g, h, i)
            return value + acc[g, ch, i] if g > 1 else value

        def body(i):
            def go():
                parts[p % 2, ch, i] = result(i).astype(jnp.bfloat16)
                part_copy(p, ch, i).start()
            live(g, h, i, go)

        each_row(body)
        inbox[p, ch, pc] = result(pc).astype(jnp.bfloat16)

    def finish(p):
        if p == 0:
            return first_settle()
        g = (p + 1) // 2
        h = g if p % 2 == 0 else g - 1
        for ch in range(CHUNKS):
            each_row(lambda i: live(g, h, i, lambda: part_copy(p, ch, i).wait_send()))

    def later(g, h):
        for ch in range(CHUNKS):
            x = solved[h, pr, ch]

            def body(i):
                value = dot_nt(x, tiles[pair(g, h), i]) * front_bit(g, h, i)
                acc[g, ch, i] = value if h == 0 else acc[g, ch, i] + value

            each_row(body)
            body(pc)

    def share_copies(g, ch):
        return [
            remote(solved.at[g, pr, ch], solved.at[g, pr, ch], share_send.at[g, ch, s],
                   share_recv.at[g, ch, pr], s, pc)
            for s in [lax.rem(pr + k, n_prow) for k in range(1, n_prow)]
        ]

    def reduce(p, ch):
        def add(source, total):
            own = source == pc
            if p == 0:
                own = own & (home == pr)
            pl.when(jnp.logical_not(own))(
                lambda: arrived(inbox.at[p, ch, source], part_recv.at[p, ch, source])
            )
            return total + inbox[p, ch, source].astype(jnp.float32)

        total = jnp.zeros((rows, size), jnp.float32)
        g = (p + 1) // 2
        if p % 2 == 0:
            x = lax.fori_loop(0, pc + 1, add, total).astype(jnp.bfloat16)
            solved[g, pr, ch] = x
            for copy in share_copies(g, ch):
                copy.start()
            return x
        total = lax.fori_loop(0, n_pcol, add, total)
        start = pl.multiple_of((pr * CHUNKS + ch) * rows, rows)
        return (turned[g, pl.ds(start, rows), :].astype(jnp.float32) - total).astype(jnp.bfloat16)

    def write(g):
        for ch in range(CHUNKS):
            for k in range(1, n_prow):
                s = lax.rem(pr + k, n_prow)
                arrived(solved.at[g, s, ch], share_recv.at[g, ch, s])
        out[g, 0] = solved[g].reshape(width, size).astype(jnp.float32).T.astype(jnp.bfloat16)
        for ch in range(CHUNKS):
            for copy in share_copies(g, ch):
                copy.wait_send()

    def turn(g):
        turned[g] = flat[g].astype(jnp.float32).T.astype(jnp.bfloat16)

    send_at = {}
    for g in range(1, levels):
        for h in range(g + 1):
            phase = 2 * g - 2 if h == g else 2 * g - 3 if h == g - 1 else 2 * g - 4
            send_at.setdefault(max(0, phase), []).append((g, h))

    flat_copy.wait()
    turn(0)
    for r in range(per_level):
        load(0, 0, r).wait()
    pl.semaphore_wait(barrier, n_prow - 1 + n_pcol - 1 + (n_prow - 1) * per_level)
    for p in range(phases):
        if p == 0:
            issue(1, 0)
            first_phase()
        else:
            for ch in range(CHUNKS):
                products(p, ch, reduce(p - 1, ch))
        for g, h in send_at.get(p, []):
            if (g, h) != (1, 0):
                issue(g, h)
        if p == 0:
            for g in range(1, levels):
                turn(g)
        else:
            finish(p - 1)
        g = (p + 2) // 2
        if p % 2 == 0 and g < levels:
            for h in range(g):
                relay(g, h)
            for h in range(g):
                collect(g, h)
                if h < g - 1:
                    later(g, h)
            if p > 0:
                write(p // 2 - 1)
        elif p % 2 == 1:
            relay(g, g)
            collect(g, g)
    finish(phases - 1)
    for g in range(1, levels):
        for h in range(g + 1):
            settle(g, h)
    if levels > 1:
        write(levels - 2)
    for ch in range(CHUNKS):
        reduce(phases - 1, ch)
    write(levels - 1)


def local(n_prow, n_pcol, factor, right_side, node_blocks, front_mask):
    levels, _, size, width = right_side.shape
    per_level = n_pcol // n_prow
    rows = width // n_prow // CHUNKS
    phases = 2 * levels - 1
    count = levels * (levels + 1) // 2
    relays = max(1, n_prow // 2 - 1)
    anywhere = pl.BlockSpec(memory_space=pl.ANY)
    smem = pl.BlockSpec(memory_space=pltpu.SMEM)
    dma = pltpu.SemaphoreType.DMA
    bf16 = jnp.bfloat16
    return pl.pallas_call(
        functools.partial(kernel, n_prow, n_pcol),
        out_shape=jax.ShapeDtypeStruct(right_side.shape, bf16),
        in_specs=[anywhere, anywhere, smem, smem],
        out_specs=pl.BlockSpec(memory_space=pltpu.VMEM),
        scratch_shapes=[
            pltpu.VMEM((count, n_pcol, size, size), bf16),
            pltpu.VMEM((levels, size, width), bf16),
            pltpu.VMEM((levels, width, size), bf16),
            pltpu.VMEM((levels, CHUNKS, n_pcol, rows, size), jnp.float32),
            pltpu.VMEM((per_level, n_prow, CHUNKS, rows, size), bf16),
            pltpu.VMEM((2, CHUNKS, n_pcol, rows, size), bf16),
            pltpu.VMEM((phases, CHUNKS, n_pcol, rows, size), bf16),
            pltpu.VMEM((levels, n_prow, CHUNKS, rows, size), bf16),
            dma((count, per_level)),
            dma,
            dma((count, per_level, n_prow // 2)),
            dma((count, per_level, relays)),
            dma((count, n_pcol)),
            dma((per_level, n_prow, CHUNKS)),
            dma((2, CHUNKS, n_pcol)),
            dma((phases, CHUNKS, n_pcol)),
            dma((levels, CHUNKS, n_prow)),
            dma((levels, CHUNKS, n_prow)),
        ],
        compiler_params=pltpu.CompilerParams(
            collective_id=0, has_side_effects=True, vmem_limit_bytes=60 * 2**20
        ),
    )(factor, right_side, node_blocks, front_mask)


def solution(mesh):
    in_specs = (P(None, "prow", None, "pcol", None, None), P(None, "pcol", None, None), P(), P())
    out_specs = P(None, "pcol", None, None)
    return jax.shard_map(
        functools.partial(local, mesh.shape["prow"], mesh.shape["pcol"]),
        mesh=mesh, in_specs=in_specs, out_specs=out_specs, check_vma=False,
    )
```

time: 649 us -> 79.8 us (0.12)
  waiting for transfers between devices: 507 us -> 0 us
  blocking collectives: 84 us -> 0 us
  Pallas kernels: 0 us -> 77.6 us
  local copies, waits for them, and re-layouts: 15.9 us -> 1.87 us
  between operations: 13.6 us -> 0.01 us
  starting transfers between devices: 11.9 us -> 0 us
  matrix products: 11.3 us -> 0 us
    unnamed x14 -> x0, waiting for transfers between devices: 485 us -> none
    pallas_call x0 -> x1, Pallas kernels: none -> 77.6 us  [local(): pl.pallas_call(functools.partial(kernel, n_prow, n_pcol), out_shape=jax.S...]
    all_to_all x4 -> x0, blocking collectives: 44.7 us -> none  [the longest x3 33.5 us: local(): lax.all_to_all(stacked.reshape(pcol_count, 1, piece_rows, rhs_width).asty...]
    all_gather x7 -> x0, blocking collectives: 39.3 us -> none  [the longest x4 23.1 us: local(): lax.all_gather(mine_solved.reshape(level_rows, 1, piece_rows, rhs_width),...]
    all_to_all x3 -> x0, waiting for transfers between devices: 22 us -> none  [local(): lax.all_to_all(stacked_solved.reshape(pcol_count, 1, piece_rows, rhs_widt...]
    unnamed x17 -> x1, local copies, waits for them, and re-layouts: 14.4 us -> 1.87 us
    all_to_all x3 -> x0, starting transfers between devices: 11.7 us -> none  [local(): lax.all_to_all(stacked_solved.reshape(pcol_count, 1, piece_rows, rhs_widt...]
    dot_general x7 -> x0, matrix products: 11.3 us -> none  [panel_products(): jnp.einsum('nxy,yw->nxw', tile_stack, vector, preferred_element_type=jnp....]
  transfers between devices with their start and end apart: 10 -> 0, of which waited for: 10 -> 0; matrix products, arithmetic and copies ran while one was open for 0% -> 0% of each run, Pallas kernels for 0% -> 0%
where the time goes in v2:
time: 79.8 us; the launch traced here: 79.5 us
  Pallas kernels  77.6 us (97%)
  local copies, waits for them, and re-layouts  1.87 us (2%)
    pallas_call x1, Pallas kernels, local(): pl.pallas_call(functools.partial(kernel, n_prow, n_pcol), out_shape=jax.S...  77.6 us
    unnamed x1, local copies, waits for them, and re-layouts  1.87 us

profile of v2, /device:TPU:0, one launch (start us, length us, event | category | flops | bytes accessed | tf_op | source)
XLA Modules:
  0.0 79.5 jit_solution(14606801352476891993)
XLA Ops:
  0.0 77.6 %shard_map.46 = bf16[4,1,256,256]{3,2,1,0:T(8,128)(2,1)} custom-call(bf16[8,1,4,1,256,256]{5,4,3,2,1,0:T(8,128)(2,1)} %factor.1, bf16[4,1,256,256]{3,2,1,0:T(8,128)(2,1)} %right.1, s32[15]{0:T(128)} %nodes.1, s32[15,32]{1,0:T(8,128)} %front.1), custom_call_target="tpu_custom_call" | custom-call | tf_op jit(solution)/shard_map/pallas_call | solution.py:360
  77.6 1.9 %copy.6 = bf16[4,1,256,256]{3,2,1,0:T(8,128)(2,1)} copy(bf16[4,1,256,256]{3,2,1,0:T(8,128)(2,1)} %shard_map.46) | data formatting | bytes 1048576

commit v3 on v2

--- a/solution.py
+++ b/solution.py
@@ -9,6 +9,7 @@
 
 MESH = pl.DeviceIdType.MESH
 CHUNKS = 2
+BATCH = 4
 
 
 def pair(g, h):
@@ -178,11 +179,11 @@
     def first_phase():
         for r in far:
             i = place(r)
+            value = dot_nt(turned[0], tiles[0, i]) * diag_bit(0, i)
+            first[r] = value.astype(jnp.bfloat16).reshape(n_prow, CHUNKS, rows, size)
 
             @pl.when(i >= pc)
             def _():
-                value = dot_nt(turned[0], tiles[0, i]) * diag_bit(0, i)
-                first[r] = value.astype(jnp.bfloat16).reshape(n_prow, CHUNKS, rows, size)
                 for ch in range(CHUNKS):
                     def stay(ch=ch):
                         inbox[0, ch, pc] = first[r, pr, ch]
@@ -199,21 +200,22 @@
         return remote(parts.at[p % 2, ch, i], inbox.at[p, ch, pc], part_send.at[p % 2, ch, i],
                       part_recv.at[p, ch, pc], pr, i)
 
-    def each_row(body):
-        def step(k):
-            return lax.rem(pc + n_pcol // 2 + k, n_pcol)
+    def each_group(body):
+        def group(k):
+            return [lax.rem(pc + n_pcol // 2 + k * BATCH + m, n_pcol) for m in range(BATCH)]
 
         if n_pcol <= 8:
-            for k in range(n_pcol):
-                if k != n_pcol // 2:
-                    body(step(k))
+            for k in range(n_pcol // BATCH):
+                body(group(k))
         else:
             def loop(k, carry):
-                i = step(k)
-                pl.when(i != pc)(lambda: body(i))
+                body(group(k))
                 return carry
 
-            lax.fori_loop(0, n_pcol, loop, 0)
+            lax.fori_loop(0, n_pcol // BATCH, loop, 0)
+
+    def goes(g, h, i):
+        return (i != pc) & (i >= pc) if g == h else i != pc
 
     def products(p, ch, x):
         g = (p + 1) // 2
@@ -224,16 +226,17 @@
             if p % 2 == 0:
                 return value * diag_bit(g, i)
             value = value * front_bit(g, h, i)
-            return value + acc[g, ch, i] if g > 1 else value
-
-        def body(i):
-            def go():
-                parts[p % 2, ch, i] = result(i).astype(jnp.bfloat16)
-                part_copy(p, ch, i).start()
-            live(g, h, i, go)
-
-        each_row(body)
-        inbox[p, ch, pc] = result(pc).astype(jnp.bfloat16)
+            return value + acc[g, i, pl.ds(ch * rows, rows)] if g > 1 else value
+
+        def body(group):
+            values = [result(i).astype(jnp.bfloat16) for i in group]
+            for i, value in zip(group, values):
+                parts[p % 2, ch, i] = value
+            for i in group:
+                pl.when(goes(g, h, i))(part_copy(p, ch, i).start)
+
+        each_group(body)
+        inbox[p, ch, pc] = parts[p % 2, ch, pc]
 
     def finish(p):
         if p == 0:
@@ -241,18 +244,20 @@
         g = (p + 1) // 2
         h = g if p % 2 == 0 else g - 1
         for ch in range(CHUNKS):
-            each_row(lambda i: live(g, h, i, lambda: part_copy(p, ch, i).wait_send()))
+            def body(group):
+                for i in group:
+                    pl.when(goes(g, h, i))(part_copy(p, ch, i).wait_send)
+            each_group(body)
 
     def later(g, h):
-        for ch in range(CHUNKS):
-            x = solved[h, pr, ch]
-
-            def body(i):
-                value = dot_nt(x, tiles[pair(g, h), i]) * front_bit(g, h, i)
-                acc[g, ch, i] = value if h == 0 else acc[g, ch, i] + value
-
-            each_row(body)
-            body(pc)
+        x = solved[h, pr].reshape(CHUNKS * rows, size)
+
+        def body(group):
+            values = [dot_nt(x, tiles[pair(g, h), i]) * front_bit(g, h, i) for i in group]
+            for i, value in zip(group, values):
+                acc[g, i] = value if h == 0 else acc[g, i] + value
+
+        each_group(body)
 
     def share_copies(g, ch):
         return [
@@ -324,17 +329,20 @@
             finish(p - 1)
         g = (p + 2) // 2
         if p % 2 == 0 and g < levels:
-            for h in range(g):
-                relay(g, h)
-            for h in range(g):
-                collect(g, h)
-                if h < g - 1:
-                    later(g, h)
-            if p > 0:
-                write(p // 2 - 1)
+            relay(g, g - 1)
+            collect(g, g - 1)
+            if g > 1:
+                relay(g, g - 2)
+                collect(g, g - 2)
+                later(g, g - 2)
+                write(g - 2)
         elif p % 2 == 1:
             relay(g, g)
             collect(g, g)
+            for h in range(g - 1 if g + 1 < levels else 0):
+                relay(g + 1, h)
+                collect(g + 1, h)
+                later(g + 1, h)
     finish(phases - 1)
     for g in range(1, levels):
         for h in range(g + 1):
@@ -366,7 +374,7 @@
             pltpu.VMEM((count, n_pcol, size, size), bf16),
             pltpu.VMEM((levels, size, width), bf16),
             pltpu.VMEM((levels, width, size), bf16),
-            pltpu.VMEM((levels, CHUNKS, n_pcol, rows, size), jnp.float32),
+            pltpu.VMEM((levels, n_pcol, CHUNKS * rows, size), jnp.float32),
             pltpu.VMEM((per_level, n_prow, CHUNKS, rows, size), bf16),
             pltpu.VMEM((2, CHUNKS, n_pcol, rows, size), bf16),
             pltpu.VMEM((phases, CHUNKS, n_pcol, rows, size), bf16),

time: 79.8 us -> 82 us (1.028)
  the two profiles are of different devices: /device:TPU:0 before, /device:TPU:27 now
where the time goes in v3:
time: 82 us; the launch traced here: 81.8 us
  Pallas kernels  79.9 us (97%)
  local copies, waits for them, and re-layouts  1.87 us (2%)
    pallas_call x1, Pallas kernels, local(): pl.pallas_call(functools.partial(kernel, n_prow, n_pcol), out_shape=jax.S...  79.9 us
    unnamed x1, local copies, waits for them, and re-layouts  1.87 us

profile of v3, /device:TPU:27, one launch (start us, length us, event | category | flops | bytes accessed | tf_op | source)
XLA Modules:
  0.0 81.8 jit_solution(7635880461181263114)
XLA Ops:
  0.0 79.9 %shard_map.46 = bf16[4,1,256,256]{3,2,1,0:T(8,128)(2,1)} custom-call(bf16[8,1,4,1,256,256]{5,4,3,2,1,0:T(8,128)(2,1)} %factor.1, bf16[4,1,256,256]{3,2,1,0:T(8,128)(2,1)} %right.1, s32[15]{0:T(128)} %nodes.1, s32[15,32]{1,0:T(8,128)} %front.1), custom_call_target="tpu_custom_call" | custom-call | tf_op jit(solution)/shard_map/pallas_call | solution.py:368
  79.9 1.9 %copy.6 = bf16[4,1,256,256]{3,2,1,0:T(8,128)(2,1)} copy(bf16[4,1,256,256]{3,2,1,0:T(8,128)(2,1)} %shard_map.46) | data formatting | bytes 1048576

commit v4 on v3

v4 whole, which is shorter than its diff:
```python
import functools

import jax
import jax.numpy as jnp
from jax import lax
from jax.experimental import pallas as pl
from jax.experimental.pallas import tpu as pltpu
from jax.sharding import PartitionSpec as P

MESH = pl.DeviceIdType.MESH
CHUNKS = 2
BATCH = 4


def pair(g, h):
    return g * (g + 1) // 2 + h


def dot_nt(a, b):
    return lax.dot_general(a, b, (((1,), (1,)), ((), ())), preferred_element_type=jnp.float32)


def kernel(
    n_prow, n_pcol, factor, right, nodes, front, out,
    own, tiles, flat, turned, acc, first, parts, inbox, mates, solved,
    load_sem, flat_sem, tile_send, relay_send, tile_recv,
    first_send, part_send, part_recv, mate_send, mate_recv, share_send, share_recv,
):
    levels, _, size, width = right.shape
    per_level = n_pcol // n_prow
    rows = width // n_prow // CHUNKS
    pairs = n_prow // 2 - 1
    phases = 2 * levels - 1
    pr = lax.axis_index("prow")
    pc = lax.axis_index("pcol")
    near = pr + 1 - 2 * lax.rem(pr, 2)
    half = n_pcol // 2
    side = pc // half
    mate = pc + 1 - 2 * lax.rem(pc, 2)
    adds = lax.rem(pc, 2) == lax.rem(pr, 2)

    def device(row, col):
        return {"prow": row, "pcol": col}

    def remote(src, dst, send, recv, row, col):
        return pltpu.make_async_remote_copy(
            src_ref=src, dst_ref=dst, send_sem=send, recv_sem=recv,
            device_id=device(row, col), device_id_type=MESH,
        )

    def arrived(slot, sem):
        remote(slot, slot, share_send.at[0, 0, 0], sem, pr, pc).wait_recv()

    barrier = pltpu.get_barrier_semaphore()
    home = lax.rem(pc, n_prow)

    def greet(row, col):
        pl.semaphore_signal(barrier, inc=1, device_id=device(row, col), device_id_type=MESH)

    for k in range(1, n_prow):
        greet(lax.rem(pr + k, n_prow), pc)
    for k in range(1, n_pcol):
        greet(pr, lax.rem(pc + k, n_pcol))

    @pl.when(home != pr)
    def _():
        for k in range(n_pcol):
            greet(home, lax.rem(pc + k, n_pcol))

    def place(r):
        return r * n_prow + pr

    def load(g, h, r):
        return pltpu.make_async_copy(
            factor.at[per_level * g + r, 0, h, 0],
            tiles.at[g, place(r)] if g == h else own.at[pair(g, h), r],
            load_sem.at[pair(g, h), r],
        )

    flat_copy = pltpu.make_async_copy(right.at[:, 0], flat, flat_sem)
    flat_copy.start()
    for g in range(levels):
        for h in range(g + 1):
            for r in range(per_level):
                load(g, h, r).start()

    ends = []
    for g in range(levels):
        base = 2 ** (levels - 1 - g) - 1
        total, ends_now = jnp.int32(0), []
        for k in range(base + 1):
            total = total + nodes[base + k]
            ends_now.append(total)
        ends.append(ends_now)

    def node(g, i):
        found = jnp.int32(2 ** (levels - 1 - g) - 1)
        for end in ends[g][:-1]:
            found = found + jnp.where(i >= end, 1, 0)
        return found

    col_node = [node(g, pc) for g in range(levels)]

    def diag_bit(g, i):
        return jnp.where((node(g, i) == col_node[g]) & (i >= pc), 1.0, 0.0).astype(jnp.float32)

    def front_bit(g, h, i):
        return front[col_node[h], g * n_pcol + i].astype(jnp.float32)

    def live(i, action):
        pl.when(i >= pc)(action)

    def tile_copies(g, r):
        i = place(r)
        targets = [lax.rem(pr + 2 * k, n_prow) for k in range(1, pairs + 1)] + [near]
        return [
            remote(factor.at[per_level * g + r, 0, g, 0], tiles.at[g, i],
                   tile_send.at[g, r, k], tile_recv.at[g, i], target, pc)
            for k, target in enumerate(targets)
        ]

    def relay_copies(g, r):
        copies = []
        for k in range(1, pairs + 1):
            i = r * n_prow + lax.rem(pr + 2 * k, n_prow)
            copies.append((i, remote(tiles.at[g, i], tiles.at[g, i], relay_send.at[g, r, k - 1],
                                     tile_recv.at[g, i], near, pc)))
        return copies

    def issue(g):
        for r in range(per_level):
            def go(r=r):
                for copy in tile_copies(g, r):
                    copy.start()
            live(place(r), go)

    def relay(g):
        for r in range(per_level):
            for i, copy in relay_copies(g, r):
                def go(i=i, copy=copy):
                    arrived(tiles.at[g, i], tile_recv.at[g, i])
                    copy.start()
                live(i, go)

    def collect(g):
        for r in range(per_level):
            load(g, g, r).wait()
            for k in range(pairs + 1):
                i = r * n_prow + lax.rem(near + 2 * k, n_prow)
                live(i, lambda i=i: arrived(tiles.at[g, i], tile_recv.at[g, i]))

    def settle(g):
        for r in range(per_level):
            def go(r=r):
                for copy in tile_copies(g, r):
                    copy.wait_send()
            live(place(r), go)
            for i, copy in relay_copies(g, r):
                live(i, copy.wait_send)

    few = per_level // 2

    def far_row(m):
        return (1 - side) * few + m

    def near_row(m):
        return side * few + m

    def row_sends(p, ch, r, keep):
        copies = []
        for k in range(n_prow):
            s = lax.rem(pr + k, n_prow)
            copy = remote(first.at[p % 2, ch, r, s], inbox.at[p, ch, pc], first_send.at[p % 2, ch, r, s],
                          part_recv.at[p, ch, pc], s, place(r))
            copies.append((copy, (place(r) != pc) if keep and k == 0 else None))
        return copies

    def each(copies, action):
        for copy, test in copies:
            if test is None:
                action(copy)
            else:
                pl.when(test)(lambda copy=copy: action(copy))

    def row_mate(p, ch, m):
        return remote(first.at[p % 2, ch, far_row(m)], mates.at[p, ch, pl.ds(m * n_prow, n_prow)],
                      mate_send.at[p % 2, ch, m], mate_recv.at[p, ch, m], pr, mate)

    def crosses(p):
        return side == 0 if p % 2 == 0 else side >= 0

    def row_products(p, ch):
        g = (p + 1) // 2
        if p == 0:
            x = turned[0].reshape(n_prow, CHUNKS, rows, size)[:, ch]
        else:
            gather(g - 1, ch)
            x = solved[g - 1, :, ch]
        x = x.reshape(n_prow * rows, size)
        for r in [far_row(m) for m in range(few)] + [near_row(m) for m in range(few)]:
            if p == 0:
                value = dot_nt(x, tiles[0, place(r)]) * diag_bit(0, place(r))
            else:
                value = dot_nt(x, own[pair(g, g - 1), r]) * front_bit(g, g - 1, place(r))
            value = value.reshape(n_prow, rows, size)
            if g > 1:
                value = value + acc[g, r, :, ch]
            first[p % 2, ch, r] = value.astype(jnp.bfloat16)
        for m in range(few):
            pl.when(crosses(p) & jnp.logical_not(adds))(row_mate(p, ch, m).start)
        for m in range(few):
            r = near_row(m)

            def go(r=r):
                each(row_sends(p, ch, r, True), lambda copy: copy.start())

                @pl.when(place(r) == pc)
                def _():
                    inbox[p, ch, pc] = first[p % 2, ch, r, pr]
            if p == 0:
                live(place(r), go)
            else:
                go()

    def row_combine(p, ch):
        @pl.when(crosses(p) & adds)
        def _():
            for m in range(few):
                r = far_row(m)
                slot = mates.at[p, ch, pl.ds(m * n_prow, n_prow)]
                arrived(slot, mate_recv.at[p, ch, m])
                total = first[p % 2, ch, r].astype(jnp.float32) + slot[...].astype(jnp.float32)
                first[p % 2, ch, r] = total.astype(jnp.bfloat16)
                each(row_sends(p, ch, r, False), lambda copy: copy.start())

    def row_finish(p, ch):
        for m in range(few):
            r = near_row(m)

            def go(r=r):
                each(row_sends(p, ch, r, True), lambda copy: copy.wait_send())
            if p == 0:
                live(place(r), go)
            else:
                go()
            pl.when(crosses(p) & jnp.logical_not(adds))(row_mate(p, ch, m).wait_send)

            @pl.when(crosses(p) & adds)
            def _():
                each(row_sends(p, ch, far_row(m), False), lambda copy: copy.wait_send())

    def part_copy(p, ch, i):
        return remote(parts.at[p // 2 % 2, ch, i], inbox.at[p, ch, pc], part_send.at[p // 2 % 2, ch, i],
                      part_recv.at[p, ch, pc], pr, i)

    def part_mate(p, ch, m):
        return remote(parts.at[p // 2 % 2, ch, half + 2 * m + lax.rem(mate, 2)], mates.at[p, ch, m],
                      mate_send.at[p % 2, ch, m], mate_recv.at[p, ch, m], pr, mate)

    def column_products(p, ch, x):
        g = p // 2

        def batch(base):
            for i in [base + m for m in range(BATCH)]:
                value = dot_nt(x, tiles[g, i]) * diag_bit(g, i)
                parts[p // 2 % 2, ch, i] = value.astype(jnp.bfloat16)

        if n_pcol <= 8:
            for k in range(n_pcol // BATCH - 1, -1, -1):
                batch(k * BATCH)
        else:
            def loop(k, carry):
                batch(k * BATCH)
                return carry

            lax.fori_loop(0, n_pcol // BATCH, loop, 0)

        @pl.when(side == 0)
        def _():
            for m in range(half // 2):
                part_mate(p, ch, m).start()

        for m in range(half):
            i = side * half + m
            pl.when(i > pc)(part_copy(p, ch, i).start)
        inbox[p, ch, pc] = parts[p // 2 % 2, ch, pc]

    def column_combine(p, ch):
        @pl.when(side == 0)
        def _():
            for m in range(half // 2):
                i = half + 2 * m + lax.rem(pc, 2)
                arrived(mates.at[p, ch, m], mate_recv.at[p, ch, m])
                total = parts[p // 2 % 2, ch, i].astype(jnp.float32) + mates[p, ch, m].astype(jnp.float32)
                parts[p // 2 % 2, ch, i] = total.astype(jnp.bfloat16)
                part_copy(p, ch, i).start()

    def column_finish(p, ch):
        @pl.when(side == 0)
        def _():
            for m in range(half // 2):
                part_mate(p, ch, m).wait_send()
                part_copy(p, ch, half + 2 * m + lax.rem(pc, 2)).wait_send()

        for m in range(half):
            i = side * half + m
            pl.when(i > pc)(part_copy(p, ch, i).wait_send)

    def by_rows(p):
        return p == 0 or p % 2 == 1

    def finish(p):
        for ch in range(CHUNKS):
            (row_finish if by_rows(p) else column_finish)(p, ch)

    def later(g, h):
        x = solved[h].reshape(width, size)
        for r in range(per_level):
            load(g, h, r).wait()
            value = dot_nt(x, own[pair(g, h), r]) * front_bit(g, h, place(r))
            value = value.reshape(n_prow, CHUNKS, rows, size)
            acc[g, r] = value if h == 0 else acc[g, r] + value

    def share_copies(g, ch):
        return [
            remote(solved.at[g, pr, ch], solved.at[g, pr, ch], share_send.at[g, ch, s],
                   share_recv.at[g, ch, pr], s, pc)
            for s in [lax.rem(pr + k, n_prow) for k in range(1, n_prow)]
        ]

    def reduce(p, ch):
        def add(source, total):
            kept = source == pc
            if by_rows(p):
                kept = kept & (home == pr)
            pl.when(jnp.logical_not(kept))(
                lambda: arrived(inbox.at[p, ch, source], part_recv.at[p, ch, source])
            )
            return total + inbox[p, ch, source].astype(jnp.float32)

        total = jnp.zeros((rows, size), jnp.float32)
        near_count = lax.rem(pc, half) + 1 if p % 2 == 0 else half
        far_count = side * (half // 2) if p % 2 == 0 else half // 2
        total = lax.fori_loop(0, near_count, lambda m, t: add(side * half + m, t), total)
        total = lax.fori_loop(
            0, far_count, lambda m, t: add((1 - side) * half + 2 * m + lax.rem(pc, 2), t), total
        )
        g = (p + 1) // 2
        if p % 2 == 0:
            solved[g, pr, ch] = total.astype(jnp.bfloat16)
            for copy in share_copies(g, ch):
                copy.start()
            return None
        start = pl.multiple_of((pr * CHUNKS + ch) * rows, rows)
        return (turned[g, pl.ds(start, rows), :].astype(jnp.float32) - total).astype(jnp.bfloat16)

    def gather(g, ch):
        for k in range(1, n_prow):
            s = lax.rem(pr + k, n_prow)
            arrived(solved.at[g, s, ch], share_recv.at[g, ch, s])

    def write(g):
        out[g, 0] = solved[g].reshape(width, size).astype(jnp.float32).T.astype(jnp.bfloat16)
        for ch in range(CHUNKS):
            for copy in share_copies(g, ch):
                copy.wait_send()

    def turn(g):
        turned[g] = flat[g].astype(jnp.float32).T.astype(jnp.bfloat16)

    flat_copy.wait()
    turn(0)
    for r in range(per_level):
        load(0, 0, r).wait()
    pl.semaphore_wait(barrier, n_prow - 1 + n_pcol - 1 + (n_prow - 1) * per_level)
    for p in range(phases):
        g = (p + 1) // 2
        if p % 2 == 1:
            for r in range(per_level):
                load(g, g - 1, r).wait()
        if p > 0 and p % 2 == 0:
            collect(g)
        if p % 2 == 1:
            for ch in range(CHUNKS):
                reduce(p - 1, ch)
        for ch in range(CHUNKS):
            if by_rows(p):
                row_products(p, ch)
            else:
                column_products(p, ch, reduce(p - 1, ch))
        for ch in range(CHUNKS):
            (row_combine if by_rows(p) else column_combine)(p, ch)
        if p == 0:
            issue(1)
            for level in range(1, levels):
                turn(level)
        else:
            finish(p - 1)
        if p % 2 == 1:
            if g + 1 < levels:
                issue(g + 1)
            relay(g)
            if g > 1 and g + 1 < levels:
                for h in range(g - 1):
                    later(g + 1, h)
            write(g - 1)
        elif 0 < g < levels - 1:
            later(g + 1, g - 1)
    finish(phases - 1)
    for g in range(1, levels):
        settle(g)
    for ch in range(CHUNKS):
        reduce(phases - 1, ch)
    for ch in range(CHUNKS):
        gather(levels - 1, ch)
    write(levels - 1)


def local(n_prow, n_pcol, factor, right_side, node_blocks, front_mask):
    levels, _, size, width = right_side.shape
    per_level = n_pcol // n_prow
    rows = width // n_prow // CHUNKS
    phases = 2 * levels - 1
    count = levels * (levels + 1) // 2
    relays = max(1, n_prow // 2 - 1)
    anywhere = pl.BlockSpec(memory_space=pl.ANY)
    smem = pl.BlockSpec(memory_space=pltpu.SMEM)
    dma = pltpu.SemaphoreType.DMA
    bf16 = jnp.bfloat16
    return pl.pallas_call(
        functools.partial(kernel, n_prow, n_pcol),
        out_shape=jax.ShapeDtypeStruct(right_side.shape, bf16),
        in_specs=[anywhere, anywhere, smem, smem],
        out_specs=pl.BlockSpec(memory_space=pltpu.VMEM),
        scratch_shapes=[
            pltpu.VMEM((count, per_level, size, size), bf16),
            pltpu.VMEM((levels, n_pcol, size, size), bf16),
            pltpu.VMEM((levels, size, width), bf16),
            pltpu.VMEM((levels, width, size), bf16),
            pltpu.VMEM((levels, per_level, n_prow, CHUNKS, rows, size), jnp.float32),
            pltpu.VMEM((2, CHUNKS, per_level, n_prow, rows, size), bf16),
            pltpu.VMEM((2, CHUNKS, n_pcol, rows, size), bf16),
            pltpu.VMEM((phases, CHUNKS, n_pcol, rows, size), bf16),
            pltpu.VMEM((phases, CHUNKS, n_pcol // 2, rows, size), bf16),
            pltpu.VMEM((levels, n_prow, CHUNKS, rows, size), bf16),
            dma((count, per_level)),
            dma,
            dma((levels, per_level, n_prow // 2)),
            dma((levels, per_level, relays)),
            dma((levels, n_pcol)),
            dma((2, CHUNKS, per_level, n_prow)),
            dma((2, CHUNKS, n_pcol)),
            dma((phases, CHUNKS, n_pcol)),
            dma((2, CHUNKS, n_pcol // 2)),
            dma((phases, CHUNKS, n_pcol // 2)),
            dma((levels, CHUNKS, n_prow)),
            dma((levels, CHUNKS, n_prow)),
        ],
        compiler_params=pltpu.CompilerParams(
            collective_id=0, has_side_effects=True, vmem_limit_bytes=60 * 2**20
        ),
    )(factor, right_side, node_blocks, front_mask)


def solution(mesh):
    in_specs = (P(None, "prow", None, "pcol", None, None), P(None, "pcol", None, None), P(), P())
    out_specs = P(None, "pcol", None, None)
    return jax.shard_map(
        functools.partial(local, mesh.shape["prow"], mesh.shape["pcol"]),
        mesh=mesh, in_specs=in_specs, out_specs=out_specs, check_vma=False,
    )
```

time: 82 us -> 76.7 us (0.935)
  the two profiles are of different devices: /device:TPU:27 before, /device:TPU:0 now
where the time goes in v4:
time: 76.7 us; the launch traced here: 76.4 us
  Pallas kernels  74.6 us (97%)
  local copies, waits for them, and re-layouts  1.87 us (2%)
    pallas_call x1, Pallas kernels, local(): pl.pallas_call(functools.partial(kernel, n_prow, n_pcol), out_shape=jax.S...  74.6 us
    unnamed x1, local copies, waits for them, and re-layouts  1.87 us

profile of v4, /device:TPU:0, one launch (start us, length us, event | category | flops | bytes accessed | tf_op | source)
XLA Modules:
  0.0 76.4 jit_solution(11075337285173160054)
XLA Ops:
  0.0 74.6 %shard_map.46 = bf16[4,1,256,256]{3,2,1,0:T(8,128)(2,1)} custom-call(bf16[8,1,4,1,256,256]{5,4,3,2,1,0:T(8,128)(2,1)} %factor.1, bf16[4,1,256,256]{3,2,1,0:T(8,128)(2,1)} %right.1, s32[15]{0:T(128)} %nodes.1, s32[15,32]{1,0:T(8,128)} %front.1), custom_call_target="tpu_custom_call" | custom-call | tf_op jit(solution)/shard_map/pallas_call | solution.py:430
  74.6 1.9 %copy.6 = bf16[4,1,256,256]{3,2,1,0:T(8,128)(2,1)} copy(bf16[4,1,256,256]{3,2,1,0:T(8,128)(2,1)} %shard_map.46) | data formatting | bytes 1048576

commit v5 on v4

--- a/solution.py
+++ b/solution.py
@@ -22,9 +22,9 @@
 
 def kernel(
     n_prow, n_pcol, factor, right, nodes, front, out,
-    own, tiles, flat, turned, acc, first, parts, inbox, mates, solved,
+    own, tiles, flat, turned, acc, first, parts, inbox, solved,
     load_sem, flat_sem, tile_send, relay_send, tile_recv,
-    first_send, part_send, part_recv, mate_send, mate_recv, share_send, share_recv,
+    first_send, part_send, part_recv, share_send, share_recv,
 ):
     levels, _, size, width = right.shape
     per_level = n_pcol // n_prow
@@ -34,10 +34,6 @@
     pr = lax.axis_index("prow")
     pc = lax.axis_index("pcol")
     near = pr + 1 - 2 * lax.rem(pr, 2)
-    half = n_pcol // 2
-    side = pc // half
-    mate = pc + 1 - 2 * lax.rem(pc, 2)
-    adds = lax.rem(pc, 2) == lax.rem(pr, 2)
 
     def device(row, col):
         return {"prow": row, "pcol": col}
@@ -158,21 +154,15 @@
             for i, copy in relay_copies(g, r):
                 live(i, copy.wait_send)
 
-    few = per_level // 2
-
-    def far_row(m):
-        return (1 - side) * few + m
-
-    def near_row(m):
-        return side * few + m
-
-    def row_sends(p, ch, r, keep):
+    far = [lax.rem(pc // n_prow + 1 + k, per_level) for k in range(per_level)]
+
+    def row_sends(p, ch, r):
         copies = []
         for k in range(n_prow):
             s = lax.rem(pr + k, n_prow)
             copy = remote(first.at[p % 2, ch, r, s], inbox.at[p, ch, pc], first_send.at[p % 2, ch, r, s],
                           part_recv.at[p, ch, pc], s, place(r))
-            copies.append((copy, (place(r) != pc) if keep and k == 0 else None))
+            copies.append((copy, (place(r) != pc) if k == 0 else None))
         return copies
 
     def each(copies, action):
@@ -181,13 +171,6 @@
                 action(copy)
             else:
                 pl.when(test)(lambda copy=copy: action(copy))
-
-    def row_mate(p, ch, m):
-        return remote(first.at[p % 2, ch, far_row(m)], mates.at[p, ch, pl.ds(m * n_prow, n_prow)],
-                      mate_send.at[p % 2, ch, m], mate_recv.at[p, ch, m], pr, mate)
-
-    def crosses(p):
-        return side == 0 if p % 2 == 0 else side >= 0
 
     def row_products(p, ch):
         g = (p + 1) // 2
@@ -197,7 +180,7 @@
             gather(g - 1, ch)
             x = solved[g - 1, :, ch]
         x = x.reshape(n_prow * rows, size)
-        for r in [far_row(m) for m in range(few)] + [near_row(m) for m in range(few)]:
+        for r in far:
             if p == 0:
                 value = dot_nt(x, tiles[0, place(r)]) * diag_bit(0, place(r))
             else:
@@ -206,13 +189,11 @@
             if g > 1:
                 value = value + acc[g, r, :, ch]
             first[p % 2, ch, r] = value.astype(jnp.bfloat16)
-        for m in range(few):
-            pl.when(crosses(p) & jnp.logical_not(adds))(row_mate(p, ch, m).start)
-        for m in range(few):
-            r = near_row(m)
-
+        if p == 0 and ch == 0:
+            pl.semaphore_wait(barrier, n_prow - 1 + n_pcol - 1 + (n_prow - 1) * per_level)
+        for r in far:
             def go(r=r):
-                each(row_sends(p, ch, r, True), lambda copy: copy.start())
+                each(row_sends(p, ch, r), lambda copy: copy.start())
 
                 @pl.when(place(r) == pc)
                 def _():
@@ -222,40 +203,18 @@
             else:
                 go()
 
-    def row_combine(p, ch):
-        @pl.when(crosses(p) & adds)
-        def _():
-            for m in range(few):
-                r = far_row(m)
-                slot = mates.at[p, ch, pl.ds(m * n_prow, n_prow)]
-                arrived(slot, mate_recv.at[p, ch, m])
-                total = first[p % 2, ch, r].astype(jnp.float32) + slot[...].astype(jnp.float32)
-                first[p % 2, ch, r] = total.astype(jnp.bfloat16)
-                each(row_sends(p, ch, r, False), lambda copy: copy.start())
-
     def row_finish(p, ch):
-        for m in range(few):
-            r = near_row(m)
-
+        for r in far:
             def go(r=r):
-                each(row_sends(p, ch, r, True), lambda copy: copy.wait_send())
+                each(row_sends(p, ch, r), lambda copy: copy.wait_send())
             if p == 0:
                 live(place(r), go)
             else:
                 go()
-            pl.when(crosses(p) & jnp.logical_not(adds))(row_mate(p, ch, m).wait_send)
-
-            @pl.when(crosses(p) & adds)
-            def _():
-                each(row_sends(p, ch, far_row(m), False), lambda copy: copy.wait_send())
 
     def part_copy(p, ch, i):
         return remote(parts.at[p // 2 % 2, ch, i], inbox.at[p, ch, pc], part_send.at[p // 2 % 2, ch, i],
                       part_recv.at[p, ch, pc], pr, i)
-
-    def part_mate(p, ch, m):
-        return remote(parts.at[p // 2 % 2, ch, half + 2 * m + lax.rem(mate, 2)], mates.at[p, ch, m],
-                      mate_send.at[p % 2, ch, m], mate_recv.at[p, ch, m], pr, mate)
 
     def column_products(p, ch, x):
         g = p // 2
@@ -275,35 +234,12 @@
 
             lax.fori_loop(0, n_pcol // BATCH, loop, 0)
 
-        @pl.when(side == 0)
-        def _():
-            for m in range(half // 2):
-                part_mate(p, ch, m).start()
-
-        for m in range(half):
-            i = side * half + m
+        for i in range(n_pcol - 1, 0, -1):
             pl.when(i > pc)(part_copy(p, ch, i).start)
         inbox[p, ch, pc] = parts[p // 2 % 2, ch, pc]
 
-    def column_combine(p, ch):
-        @pl.when(side == 0)
-        def _():
-            for m in range(half // 2):
-                i = half + 2 * m + lax.rem(pc, 2)
-                arrived(mates.at[p, ch, m], mate_recv.at[p, ch, m])
-                total = parts[p // 2 % 2, ch, i].astype(jnp.float32) + mates[p, ch, m].astype(jnp.float32)
-                parts[p // 2 % 2, ch, i] = total.astype(jnp.bfloat16)
-                part_copy(p, ch, i).start()
-
     def column_finish(p, ch):
-        @pl.when(side == 0)
-        def _():
-            for m in range(half // 2):
-                part_mate(p, ch, m).wait_send()
-                part_copy(p, ch, half + 2 * m + lax.rem(pc, 2)).wait_send()
-
-        for m in range(half):
-            i = side * half + m
+        for i in range(n_pcol - 1, 0, -1):
             pl.when(i > pc)(part_copy(p, ch, i).wait_send)
 
     def by_rows(p):
@@ -339,12 +275,7 @@
             return total + inbox[p, ch, source].astype(jnp.float32)
 
         total = jnp.zeros((rows, size), jnp.float32)
-        near_count = lax.rem(pc, half) + 1 if p % 2 == 0 else half
-        far_count = side * (half // 2) if p % 2 == 0 else half // 2
-        total = lax.fori_loop(0, near_count, lambda m, t: add(side * half + m, t), total)
-        total = lax.fori_loop(
-            0, far_count, lambda m, t: add((1 - side) * half + 2 * m + lax.rem(pc, 2), t), total
-        )
+        total = lax.fori_loop(0, pc + 1 if p % 2 == 0 else n_pcol, add, total)
         g = (p + 1) // 2
         if p % 2 == 0:
             solved[g, pr, ch] = total.astype(jnp.bfloat16)
@@ -372,7 +303,6 @@
     turn(0)
     for r in range(per_level):
         load(0, 0, r).wait()
-    pl.semaphore_wait(barrier, n_prow - 1 + n_pcol - 1 + (n_prow - 1) * per_level)
     for p in range(phases):
         g = (p + 1) // 2
         if p % 2 == 1:
@@ -388,8 +318,6 @@
                 row_products(p, ch)
             else:
                 column_products(p, ch, reduce(p - 1, ch))
-        for ch in range(CHUNKS):
-            (row_combine if by_rows(p) else column_combine)(p, ch)
         if p == 0:
             issue(1)
             for level in range(1, levels):
@@ -441,7 +369,6 @@
             pltpu.VMEM((2, CHUNKS, per_level, n_prow, rows, size), bf16),
             pltpu.VMEM((2, CHUNKS, n_pcol, rows, size), bf16),
             pltpu.VMEM((phases, CHUNKS, n_pcol, rows, size), bf16),
-            pltpu.VMEM((phases, CHUNKS, n_pcol // 2, rows, size), bf16),
             pltpu.VMEM((levels, n_prow, CHUNKS, rows, size), bf16),
             dma((count, per_level)),
             dma,
@@ -451,8 +378,6 @@
             dma((2, CHUNKS, per_level, n_prow)),
             dma((2, CHUNKS, n_pcol)),
             dma((phases, CHUNKS, n_pcol)),
-            dma((2, CHUNKS, n_pcol // 2)),
-            dma((phases, CHUNKS, n_pcol // 2)),
             dma((levels, CHUNKS, n_prow)),
             dma((levels, CHUNKS, n_prow)),
         ],

time: 76.7 us -> 77.9 us (1.016)
  Pallas kernels: 74.6 us -> 75.8 us
    pallas_call x1, Pallas kernels: 74.6 us -> 75.8 us  [local(): pl.pallas_call(functools.partial(kernel, n_prow, n_pcol), out_shape=jax.S...]
where the time goes in v5:
time: 77.9 us; the launch traced here: 77.7 us
  Pallas kernels  75.8 us (97%)
  local copies, waits for them, and re-layouts  1.87 us (2%)
    pallas_call x1, Pallas kernels, local(): pl.pallas_call(functools.partial(kernel, n_prow, n_pcol), out_shape=jax.S...  75.8 us
    unnamed x1, local copies, waits for them, and re-layouts  1.87 us

profile of v5, /device:TPU:0, one launch (start us, length us, event | category | flops | bytes accessed | tf_op | source)
XLA Modules:
  0.0 77.7 jit_solution(17211926098390282658)
XLA Ops:
  0.0 75.8 %shard_map.46 = bf16[4,1,256,256]{3,2,1,0:T(8,128)(2,1)} custom-call(bf16[8,1,4,1,256,256]{5,4,3,2,1,0:T(8,128)(2,1)} %factor.1, bf16[4,1,256,256]{3,2,1,0:T(8,128)(2,1)} %right.1, s32[15]{0:T(128)} %nodes.1, s32[15,32]{1,0:T(8,128)} %front.1), custom_call_target="tpu_custom_call" | custom-call | tf_op jit(solution)/shard_map/pallas_call | solution.py:358
  75.9 1.9 %copy.6 = bf16[4,1,256,256]{3,2,1,0:T(8,128)(2,1)} copy(bf16[4,1,256,256]{3,2,1,0:T(8,128)(2,1)} %shard_map.46) | data formatting | bytes 1048576
